TPU v7x, 32 devices: a whole 2x2x4 slice. The times are simulated.
32 devices in a mesh: frame: 8 (over z, x), chan: 4 (over y, core).
Axes of the slice: x: 2, y: 2, z: 4, core: 2. Of those that a mesh axis runs over, the one named last changes fastest.
Arguments:
- query_act: bfloat16 [7040, 2240], P('frame', 'chan'), may hold values from -6 to 6
- key_act: bfloat16 [7040, 2240], P('frame', 'chan'), may hold values from -6 to 6
- value_act: bfloat16 [7040, 2240], P('frame', 'chan'), may hold values from -6 to 6
- conv_weight: bfloat16 [3, 2240, 2240], P(None, 'chan'), may hold values from -0.109375 to 0.109375
- gate_act: bfloat16 [7040, 2240], P('frame', 'chan'), may hold values from -8 to 8
Outputs:
- layer_out: bfloat16 [7040, 2240], P('frame', 'chan')
All inputs are finite; a program needn't handle non-finite values.
Results may differ from a plain program's by a relative error of at most 0.015.
Values may be sent and summed in bfloat16 or wider, within the bound.
A program may use at most 128 MiB of HBM per device.

v0:
```python
import jax
import jax.numpy as jnp
from jax import lax
from jax.sharding import PartitionSpec as P

HD = 112
TPF = 880


def entering(shard, axis, join, neutral):
    place = lax.axis_index(axis)
    gathered = lax.all_gather(shard.astype(jnp.bfloat16), axis)
    state = jnp.zeros_like(shard) + jnp.asarray(neutral, shard.dtype)

    def one(step, state):
        return join(state, lax.dynamic_index_in_dim(gathered, step, 0, False).astype(shard.dtype))

    return lax.fori_loop(0, place, one, state)


def padded(shard, sides, width):
    for axis, dim in sides:
        count, length = (lax.axis_size(axis), shard.shape[dim])
        up = [(i, (i + 1) % count) for i in range(count - 1)]
        down = [(j, i) for i, j in up]
        last = lax.slice_in_dim(shard, length - width, length, axis=dim)
        initial = lax.slice_in_dim(shard, 0, width, axis=dim)
        before = lax.ppermute(last, axis, up)
        after = lax.ppermute(initial, axis, down)
        shard = jnp.concatenate([before, shard, after], axis=dim)
    return shard


def add_states(earlier, later):
    return earlier + later


def shards(query_act, key_act, value_act, conv_weight, gate_act):
    row_count, chan_width = query_act.shape
    head_count = chan_width // HD
    frame_count = row_count // TPF
    key_feat = jnp.maximum(key_act, 0).reshape(frame_count, TPF, head_count, HD)
    value_feat = value_act.reshape(frame_count, TPF, head_count, HD)
    query_feat = jnp.maximum(query_act, 0).reshape(frame_count, TPF, head_count, HD)
    frame_state = jnp.einsum(
        "ftha,fthb->fhab", key_feat, value_feat, preferred_element_type=jnp.float32
    )
    local_prefix = jnp.cumsum(frame_state, axis=0)
    own_total = local_prefix[frame_count - 1]
    earlier = entering(own_total, "frame", add_states, jnp.zeros_like(own_total))
    prefix_state = (local_prefix + earlier[None]).astype(jnp.bfloat16)
    readout = jnp.einsum(
        "ftha,fhab->fthb", query_feat, prefix_state, preferred_element_type=jnp.float32
    )
    scale_inv = lax.rsqrt(jnp.mean(readout * readout, axis=-1, keepdims=True) + 1e-06)
    attended = (readout * scale_inv).astype(jnp.bfloat16).reshape(row_count, chan_width)
    with_rims = padded(attended, (("frame", 0),), TPF)
    partials = jnp.dot(with_rims[0:row_count], conv_weight[0], preferred_element_type=jnp.float32)
    partials = partials + jnp.dot(
        with_rims[TPF : TPF + row_count], conv_weight[1], preferred_element_type=jnp.float32
    )
    partials = partials + jnp.dot(
        with_rims[2 * TPF : 2 * TPF + row_count], conv_weight[2], preferred_element_type=jnp.float32
    )
    conv_out = lax.psum_scatter(
        partials.astype(jnp.bfloat16), "chan", scatter_dimension=1, tiled=True
    ).astype(jnp.float32)
    gate_value = jax.nn.silu(gate_act.astype(jnp.float32))
    return (conv_out * gate_value).astype(jnp.bfloat16)


def solution(mesh):
    return jax.shard_map(
        shards,
        mesh=mesh,
        in_specs=(
            P("frame", "chan"),
            P("frame", "chan"),
            P("frame", "chan"),
            P(None, "chan", None),
            P("frame", "chan"),
        ),
        out_specs=P("frame", "chan"),
        check_vma=False,
    )
```

profile of v0, /device:TPU:16, one launch (start us, length us, event | category | flops | bytes accessed | tf_op | source)
XLA Modules:
  0.0 152.9 jit_solution(11854023369550423909)
XLA Ops:
  6.5 0.0 copy-start
  6.5 0.0 copy-start.2
  6.5 0.0 reduce-scatter.2.cloned.1.call-start
  6.5 1.4 broadcast_maximum_fusion
  8.0 0.2 copy-done.2
  8.1 0.1 broadcast_maximum_fusion.1
  8.2 0.1 copy-done
  8.3 1.2 fusion.19
  9.5 29.9 %all-gather = bf16[40,112,112]{2,1,0:T(8,128)(2,1)S(1)} all-gather(bf16[5,112,112]{2,1,0:T(8,128)(2,1)S(1)} %get-tuple-element.37), channel_id=2, replica_groups=mesh['frame'=8,'chan'=4] {'frame'}, dimensions={0}, use_global_device_ids=true | all-gather | bytes 1128960 | tf_op jit(solution)/shard_map/all_gather | solution.py:12
  39.5 0.3 while.10
  39.8 1.5 fusion.15
  41.3 0.1 fusion.16
  41.4 0.0 slice-start
  41.4 0.0 slice-start.1
  41.4 5.1 %collective-permute-start = (bf16[880,560]{0,1:T(8,128)(2,1)S(1)}, bf16[880,560]{0,1:T(8,128)(2,1)S(1)}, u32[]{:S(2)}, u32[]{:S(2)}) collective-permute-start(bf16[880,560]{0,1:T(8,128)(2,1)S(1)} %bitcast.40), channel_id=1, source_target_pairs={{0,4},{4,8},{8,12},{12,16},{16,20},{20,24},{24,28},{1,5},{5,9},{9,... | collective-permute-start | bytes 2956808 | tf_op jit(solution)/shard_map/ppermute | solution.py:28
  46.6 2.3 %collective-permute-start.1 = (bf16[880,560]{0,1:T(8,128)(2,1)S(1)}, bf16[880,560]{0,1:T(8,128)(2,1)S(1)}, u32[]{:S(2)}, u32[]{:S(2)}) collective-permute-start(bf16[880,560]{0,1:T(8,128)(2,1)S(1)} %bitcast.41), channel_id=1, source_target_pairs={{4,0},{8,4},{12,8},{16,12},{20,16},{24,20},{28,24},{5,1},{9,5},{13... | collective-permute-start | bytes 2956808 | tf_op jit(solution)/shard_map/ppermute | solution.py:29
  48.9 5.6 %fusion.4 = f32[880,2240]{0,1:T(8,128)S(1)} fusion(bf16[880,560]{0,1:T(8,128)(2,1)S(1)} %bitcast.42, bf16[3,560,2240]{2,1,0:T(8,128)(2,1)} %param.10), kind=kOutput, calls=%fused_computation.4 | convolution fusion | flops 2207744000 | bytes 11450880 | tf_op jit(solution)/shard_map/dot_general | solution.py:59
  54.6 30.2 %collective-permute-done = bf16[880,560]{0,1:T(8,128)(2,1)S(1)} collective-permute-done((bf16[880,560]{0,1:T(8,128)(2,1)S(1)}, bf16[880,560]{0,1:T(8,128)(2,1)S(1)}, u32[]{:S(2)}, u32[]{:S(2)}) %collective-permute-start) | collective-permute-done | bytes 985632 | tf_op jit(solution)/shard_map/ppermute | solution.py:28
  84.8 0.0 slice-done
  84.8 0.0 slice-done.1
  84.8 5.9 %fusion.6 = f32[880,2240]{0,1:T(8,128)} fusion(bf16[880,560]{0,1:T(8,128)(2,1)S(1)} %collective-permute-done, bf16[3,560,2240]{2,1,0:T(8,128)(2,1)S(1)} %bitcast.44), kind=kOutput, calls=%fused_computation.6 | convolution fusion | flops 2207744000 | bytes 11468800 | tf_op jit(solution)/shard_map/dot_general | solution.py:58
  90.7 0.0 collective-permute-done.1
  90.7 7.9 %add_convert_fusion = bf16[880,2240]{0,1:T(8,128)(2,1)} fusion(f32[880,2240]{0,1:T(8,128)} %fusion.6, f32[880,2240]{0,1:T(8,128)S(1)} %fusion.4, bf16[880,560]{0,1:T(8,128)(2,1)S(1)} %collective-permute-done.1, bf16[3,560,2240]{2,1,0:T(8,128)(2,1)S(1)} %bitcast.44), kind=kOutput, calls=%fused_computation.1 | convolution fusion | flops 2213657600 | bytes 23439360 | tf_op jit(solution)/shard_map/dot_general | solution.py:62
  98.6 0.0 copy-start.1
  98.6 0.0 reduce-scatter.2.cloned.1.call-update
  98.6 44.6 %reduce-scatter.2.cloned.1.call-done = bf16[880,560]{0,1:T(8,128)(2,1)} async-done(((bf16[880,2240]{0,1:T(8,128)(2,1)}), bf16[880,560]{0,1:T(8,128)(2,1)}) %reduce-scatter.2.cloned.1.call-update) | async-done | bytes 985616 | tf_op jit(solution)/shard_map/reduce_scatter | solution.py:65
  143.2 0.0 copy-done.1
  143.2 2.8 %fusion.17 = bf16[880,560]{0,1:T(8,128)(2,1)} fusion(bf16[880,560]{0,1:T(8,128)(2,1)S(1)} %copy-done.1, bf16[880,560]{0,1:T(8,128)(2,1)} %reduce-scatter.2.cloned.1.call-done), kind=kLoop, calls=%fused_computation.21 | loop fusion | flops 3942400 | bytes 2956800 | tf_op jit(solution)/shard_map/convert_element_type | solution.py:69
  (7 shorter events, 0.2 us)
Async XLA Ops:
  6.5 1.8 %copy-start = (bf16[880,560]{0,1:T(8,128)(2,1)S(1)}, bf16[880,560]{0,1:T(8,128)(2,1)}, u32[]{:S(2)}) copy-start(bf16[880,560]{0,1:T(8,128)(2,1)} %param.9) | copy-start | bytes 2956804
  6.5 1.6 %copy-start.2 = (bf16[880,560]{0,1:T(8,128)(2,1)S(1)}, bf16[880,560]{0,1:T(8,128)(2,1)}, u32[]{:S(2)}) copy-start(bf16[880,560]{0,1:T(8,128)(2,1)} %param.8) | copy-start | bytes 2956804
  6.5 136.7 %reduce-scatter.2.cloned.1.call-start = ((), (), s32[]{:S(2)}) async-start(), calls=%async_computation.1 | async-start | bytes 5017600 | tf_op jit(solution)/shard_map/reduce_scatter | solution.py:65
  41.4 43.4 %slice-start = ((s8[7741440]{0:T(1024)(128)(4,1)}), s8[4194304]{0:T(1024)(128)(4,1)S(1)}, s32[]{:S(2)}) async-start(s8[7741440]{0:T(1024)(128)(4,1)} %bitcast.43), calls=%async_computation.2 | async-start | bytes 8388608
  41.4 43.4 %slice-start.1 = ((s8[7741440]{0:T(1024)(128)(4,1)}), s8[3547136]{0:T(1024)(128)(4,1)S(1)}, s32[]{:S(2)}) async-start(s8[7741440]{0:T(1024)(128)(4,1)} %bitcast.43), calls=%async_computation.3 | async-start | bytes 7094272
  41.4 43.3 %collective-permute-start = (bf16[880,560]{0,1:T(8,128)(2,1)S(1)}, bf16[880,560]{0,1:T(8,128)(2,1)S(1)}, u32[]{:S(2)}, u32[]{:S(2)}) collective-permute-start(bf16[880,560]{0,1:T(8,128)(2,1)S(1)} %bitcast.40), channel_id=1, source_target_pairs={{0,4},{4,8},{8,12},{12,16},{16,20},{20,24},{24,28},{1,5},{5,9},{9,... | collective-permute-start | bytes 2956808 | tf_op jit(solution)/shard_map/ppermute | solution.py:28
  46.6 44.1 %collective-permute-start.1 = (bf16[880,560]{0,1:T(8,128)(2,1)S(1)}, bf16[880,560]{0,1:T(8,128)(2,1)S(1)}, u32[]{:S(2)}, u32[]{:S(2)}) collective-permute-start(bf16[880,560]{0,1:T(8,128)(2,1)S(1)} %bitcast.41), channel_id=1, source_target_pairs={{4,0},{8,4},{12,8},{16,12},{20,16},{24,20},{28,24},{5,1},{9,5},{13... | collective-permute-start | bytes 2956808 | tf_op jit(solution)/shard_map/ppermute | solution.py:29
  98.6 44.6 %copy-start.1 = (bf16[880,560]{0,1:T(8,128)(2,1)S(1)}, bf16[880,560]{0,1:T(8,128)(2,1)}, u32[]{:S(2)}) copy-start(bf16[880,560]{0,1:T(8,128)(2,1)} %param.11) | copy-start | bytes 2956804
Sparse Core Ops, SparseCore 0:
  98.7 44.4 reduce-scatter.1
where the time goes:
time: 155 us; the launch traced here: 153 us
  waiting for transfers between devices  74.9 us (48%)
  blocking collectives  29.9 us (19%)
  matrix products  22.1 us (14%)
  between operations  13.5 us (9%)
  starting transfers between devices  7.47 us (5%)
  other arithmetic  4.65 us (3%)
    reduce_scatter x1, waiting for transfers between devices, shards(): lax.psum_scatter(partials.astype(jnp.bfloat16), 'chan', scatter_dimension...  44.6 us
    ppermute x1, waiting for transfers between devices, padded(): before = lax.ppermute(last, axis, up)  30.2 us
    all_gather x1, blocking collectives, entering(): gathered = lax.all_gather(shard.astype(jnp.bfloat16), axis)  29.9 us
    dot_general x1, matrix products, shards(): jnp.dot(with_rims[2 * TPF:2 * TPF + row_count], conv_weight[2], preferred...  7.94 us
    dot_general x1, matrix products, shards(): jnp.dot(with_rims[0:row_count], conv_weight[0], preferred_element_type=jn...  5.87 us
    dot_general x1, matrix products, shards(): jnp.dot(with_rims[TPF:TPF + row_count], conv_weight[1], preferred_element...  5.64 us
    ppermute x1, starting transfers between devices, padded(): before = lax.ppermute(last, axis, up)  5.14 us
  transfers between devices with their start and end apart: 3, of which 2 were waited for; matrix products, arithmetic and copies ran while one was open for 8% of the time, Pallas kernels for 0%

commit v1 on v0

v1 whole, which is shorter than its diff:
```python
import functools

import jax
import jax.numpy as jnp
from jax import lax
from jax.experimental import pallas as pl
from jax.experimental.pallas import tpu as pltpu
from jax.sharding import PartitionSpec as P

HD = 112
TPF = 880
PARTS = 2
F32 = jnp.float32
BF16 = jnp.bfloat16
MESH = pl.DeviceIdType.MESH


def kernel(
    frames,
    q_ref, k_ref, v_ref, w_hbm, g_hbm, out_ref,
    w_all, wb, wsib, gate, own_state, pair_state, chain_in, chain_out, spread, qx,
    a_own, a_sib, cross, cross_in, kept, back, back_in,
    load_sem, w_send, w_recv, x_send, x_recv, c_send, c_recv, q_send, q_recv,
    s_send, s_recv, h_send, h_recv, f_send, f_recv, y_send, y_recv, b_send, b_recv,
):
    rows, width = q_ref.shape
    half = qx.shape[0]
    chunk = half // PARTS
    shift = rows - half
    heads = width // HD
    pairs = frames // 2
    f = lax.axis_index("frame")
    m = lax.axis_index("chan")
    x = lax.rem(f, 2)
    p = f // 2
    first, last = p == 0, p == pairs - 1
    sib_m = m + 1 - 2 * lax.rem(m, 2)
    far_m = m + 2 - 4 * lax.rem(m // 2, 2)
    far_sib_m = far_m + 1 - 2 * lax.rem(far_m, 2)
    sib, far, mate = (f, sib_m), (f, far_m), (f + 1 - 2 * x, m)
    up, down = (f - 2, m), (f + 2, m)

    def remote(src, dst, send, recv, device):
        return pltpu.make_async_remote_copy(
            src_ref=src, dst_ref=dst, send_sem=send, recv_sem=recv,
            device_id=device, device_id_type=MESH,
        )

    taps = w_hbm.shape[0]
    loads = [pltpu.make_async_copy(w_hbm.at[t], w_all.at[t], load_sem.at[t]) for t in range(taps)]
    loads.append(pltpu.make_async_copy(g_hbm, gate, load_sem.at[taps]))
    for load in loads:
        load.start()

    barrier = pltpu.get_barrier_semaphore()
    for device in (sib, far, mate):
        pl.semaphore_signal(barrier, inc=1, device_id=device, device_id_type=MESH)

    @pl.when(jnp.logical_not(first))
    def _():
        pl.semaphore_signal(barrier, inc=1, device_id=up, device_id_type=MESH)

    @pl.when(jnp.logical_not(last))
    def _():
        pl.semaphore_signal(barrier, inc=1, device_id=down, device_id_type=MESH)

    col_head = lax.broadcasted_iota(jnp.int32, (HD, width), 1) // HD
    full = lax.dot_general(
        jnp.maximum(k_ref[...], 0), v_ref[...], (((0,), (0,)), ((), ())),
        preferred_element_type=F32,
    )
    state = jnp.zeros((HD, width), F32)
    for h in range(heads):
        state = jnp.where(col_head == h, full[h * HD:(h + 1) * HD, :], state)
    own_state[...] = state.astype(BF16)

    pl.semaphore_wait(barrier, 3 + jnp.where(first, 0, 1) + jnp.where(last, 0, 1))

    swap = remote(own_state, pair_state, x_send.at[0], x_recv.at[0], mate)
    swap.start()
    mate_row = pl.multiple_of((1 - x) * shift, 16)
    q_moves = [
        remote(
            q_ref.at[pl.ds(pl.multiple_of(mate_row + i * chunk, 16), chunk), :],
            qx.at[pl.ds(i * chunk, chunk), :], q_send.at[i], q_recv.at[i], mate,
        )
        for i in range(PARTS)
    ]
    for move in q_moves:
        move.start()

    for t in range(taps):
        loads[t].wait()
        for b in range(wb.shape[0]):
            wb[b, t] = w_all[t, :, b * width:(b + 1) * width]
    w_moves = [
        remote(wb.at[far_sib_m], wsib.at[1], w_send.at[0], w_recv.at[0], sib),
        remote(wb.at[sib_m], wsib.at[0], w_send.at[1], w_recv.at[1], sib),
    ]
    for move in w_moves:
        move.start()

    @pl.when(first)
    def _():
        a_own[0] = jnp.zeros((half, width), BF16)
        a_sib[0] = jnp.zeros((half, width), BF16)
        chain_in[...] = jnp.zeros((HD, width), BF16)

    @pl.when(last)
    def _():
        a_own[3] = jnp.zeros((half, width), BF16)
        a_sib[3] = jnp.zeros((half, width), BF16)

    swap.wait()
    cuts = [(0, 64), (64, HD - 64)]
    chain = [
        remote(
            chain_out.at[pl.ds(at, size), :], chain_in.at[pl.ds(at, size), :],
            c_send.at[i], c_recv.at[i], down,
        )
        for i, (at, size) in enumerate(cuts)
    ]
    for i, (at, size) in enumerate(cuts):
        @pl.when(jnp.logical_not(first))
        def _():
            chain[i].wait_recv()

        span = pl.ds(at, size)
        before = chain_in[span, :].astype(F32)
        mine = own_state[span, :].astype(F32)
        other = pair_state[span, :].astype(F32)
        low = jnp.where(x == 0, mine, other)
        chain_out[span, :] = (before + mine + other).astype(BF16)

        @pl.when(jnp.logical_not(last))
        def _():
            chain[i].start()

        own_state[span, :] = (before + low).astype(BF16)

    for j, source in enumerate((own_state, chain_out)):
        for h in range(heads):
            spread[j, h * HD:(h + 1) * HD, :] = jnp.where(col_head == h, source[...], 0)

    lanes = 128
    group = (
        lax.broadcasted_iota(jnp.int32, (width, lanes), 0) // HD
        == lax.broadcasted_iota(jnp.int32, (width, lanes), 1)
    ).astype(BF16)
    ungroup = (
        lax.broadcasted_iota(jnp.int32, (lanes, width), 1) // HD
        == lax.broadcasted_iota(jnp.int32, (lanes, width), 0)
    ).astype(BF16)

    def attend(query, prefix):
        readout = jnp.dot(jnp.maximum(query, 0), prefix, preferred_element_type=F32)
        total = jnp.dot((readout * readout).astype(BF16), group, preferred_element_type=F32)
        inverse = lax.rsqrt(total * (1.0 / HD) + 1e-06)
        coarse = inverse.astype(BF16)
        fine = (inverse - coarse.astype(F32)).astype(BF16)
        factor = jnp.dot(coarse, ungroup, preferred_element_type=F32)
        factor = factor + jnp.dot(fine, ungroup, preferred_element_type=F32)
        return (readout * factor).astype(BF16)

    def part(ref, slot, i):
        return ref.at[slot, pl.ds(pl.multiple_of(i * chunk, 16), chunk), :]

    def to_sib(slot, i):
        return remote(part(a_own, slot, i), part(a_sib, slot, i), s_send.at[slot - 1, i], s_recv.at[slot - 1, i], sib)

    def go_down(i):
        return remote(part(a_own, 2, i), part(a_own, 0, i), h_send.at[0, i], h_recv.at[0, i], down)

    def go_up(i):
        return remote(part(a_own, 1, i), part(a_own, 3, i), h_send.at[1, i], h_recv.at[1, i], up)

    def forward(j, i):
        return remote(part(a_own, 3 * j, i), part(a_sib, 3 * j, i), f_send.at[j, i], f_recv.at[j, i], sib)

    my_row = pl.multiple_of(x * shift, 16)
    for i in range(PARTS):
        span = pl.ds(i * chunk, chunk)
        mine = attend(q_ref[pl.ds(pl.multiple_of(my_row + i * chunk, 16), chunk), :], spread[x])
        a_own[1 + x, span, :] = mine
        q_moves[i].wait_recv()
        a_own[2 - x, span, :] = attend(qx[span, :], spread[1 - x])

        @pl.when(jnp.logical_not(last))
        def _():
            go_down(i).start()

        @pl.when(jnp.logical_not(first))
        def _():
            go_up(i).start()

        to_sib(1, i).start()
        to_sib(2, i).start()

    def y_move(s):
        return remote(cross.at[s], cross_in.at[s], y_send.at[s], y_recv.at[s], far)

    def b_move(i):
        return remote(back.at[i], back_in.at[i], b_send.at[i], b_recv.at[i], mate)

    def gated(total, at):
        span = pl.ds(pl.multiple_of(at, 16), chunk)
        u = gate[span, :].astype(F32)
        out_ref[span, :] = (total * (u / (1.0 + jnp.exp(-u)))).astype(BF16)

    def finish(s):
        j, i = s // PARTS, lax.rem(s, PARTS)
        y_move(s).wait_recv()
        total = kept[s] + cross_in[s].astype(F32)

        @pl.when(j == x)
        def _():
            gated(total, my_row + i * chunk)

        @pl.when(j != x)
        def _():
            back[i] = total.astype(BF16)
            b_move(i).start()

    loads[taps].wait()
    w_moves[0].wait_recv()
    w_moves[1].wait_recv()

    def step(s, carry):
        j, i = s // PARTS, lax.rem(s, PARTS)
        span = pl.ds(pl.multiple_of(i * chunk, 16), chunk)

        @pl.when(j == 0)
        def _():
            to_sib(1, i).wait_recv()
            to_sib(2, i).wait_recv()

        def dot(a, slot, w):
            return jnp.dot(a[slot, span, :], w[...], preferred_element_type=F32)

        def inner(mine, theirs):
            acc = dot(a_own, 1, mine.at[1 - j]) + dot(a_own, 2, mine.at[2 - j])
            return acc + dot(a_sib, 1, theirs.at[1 - j]) + dot(a_sib, 2, theirs.at[2 - j])

        def outer(mine, theirs):
            return dot(a_own, 3 * j, mine.at[2 * j]) + dot(a_sib, 3 * j, theirs.at[2 * j])

        has = jnp.logical_and(p + j > 0, p + j < pairs)

        @pl.when(has)
        def _():
            remote(part(a_own, 2 - j, i), part(a_own, 3 * j, i), h_send.at[j, i], h_recv.at[j, i], sib).wait_recv()
            forward(j, i).start()

        kept[s] = inner(wb.at[far_m], wsib.at[1])

        @pl.when(has)
        def _():
            forward(j, i).wait_recv()

        cross[s] = (kept[s] + outer(wb.at[far_m], wsib.at[1])).astype(BF16)
        y_move(s).start()
        kept[s] = inner(wb.at[m], wsib.at[0]) + outer(wb.at[m], wsib.at[0])

        @pl.when(s > 0)
        def _():
            finish(s - 1)

        return carry

    steps = 2 * PARTS
    lax.fori_loop(0, steps, step, 0)
    finish(steps - 1)
    for i in range(PARTS):
        b_move(i).wait_recv()
        gated(back_in[i].astype(F32), mate_row + i * chunk)

    for move in q_moves:
        move.wait_send()
    for move in w_moves:
        move.wait_send()
    for s in range(steps):
        y_move(s).wait_send()

    for i in range(PARTS):
        to_sib(1, i).wait_send()
        to_sib(2, i).wait_send()
        b_move(i).wait_send()

        @pl.when(jnp.logical_not(last))
        def _():
            go_down(i).wait_send()
            forward(1, i).wait_send()

        @pl.when(jnp.logical_not(first))
        def _():
            go_up(i).wait_send()
            forward(0, i).wait_send()

    @pl.when(jnp.logical_not(last))
    def _():
        for move in chain:
            move.wait_send()


def shards(frames, query_act, key_act, value_act, conv_weight, gate_act):
    rows, width = query_act.shape
    taps, _, outs = conv_weight.shape
    chans = outs // width
    assert rows == TPF and frames % 2 == 0 and chans == 4
    half = -(-rows // (32 * PARTS)) * 16 * PARTS
    chunk = half // PARTS
    dma = pltpu.SemaphoreType.DMA
    vmem = pl.BlockSpec(memory_space=pltpu.VMEM)
    hbm = pl.BlockSpec(memory_space=pl.ANY)
    return pl.pallas_call(
        functools.partial(kernel, frames),
        out_shape=jax.ShapeDtypeStruct((rows, width), BF16),
        in_specs=[vmem, vmem, vmem, hbm, hbm],
        out_specs=vmem,
        scratch_shapes=[
            pltpu.VMEM((taps, width, outs), BF16),
            pltpu.VMEM((chans, taps, width, width), BF16),
            pltpu.VMEM((2, taps, width, width), BF16),
            pltpu.VMEM((rows, width), BF16),
            pltpu.VMEM((HD, width), BF16),
            pltpu.VMEM((HD, width), BF16),
            pltpu.VMEM((HD, width), BF16),
            pltpu.VMEM((HD, width), BF16),
            pltpu.VMEM((2, width, width), BF16),
            pltpu.VMEM((half, width), BF16),
            pltpu.VMEM((4, half, width), BF16),
            pltpu.VMEM((4, half, width), BF16),
            pltpu.VMEM((2 * PARTS, chunk, width), BF16),
            pltpu.VMEM((2 * PARTS, chunk, width), BF16),
            pltpu.VMEM((2 * PARTS, chunk, width), F32),
            pltpu.VMEM((PARTS, chunk, width), BF16),
            pltpu.VMEM((PARTS, chunk, width), BF16),
            dma((taps + 1,)),
            dma((2,)), dma((2,)),
            dma((1,)), dma((1,)),
            dma((2,)), dma((2,)),
            dma((PARTS,)), dma((PARTS,)),
            dma((2, PARTS)), dma((2, PARTS)),
            dma((2, PARTS)), dma((2, PARTS)),
            dma((2, PARTS)), dma((2, PARTS)),
            dma((2 * PARTS,)), dma((2 * PARTS,)),
            dma((PARTS,)), dma((PARTS,)),
        ],
        compiler_params=pltpu.CompilerParams(
            collective_id=0, has_side_effects=True, vmem_limit_bytes=56 * 1024 * 1024
        ),
    )(query_act, key_act, value_act, conv_weight, gate_act)


def solution(mesh):
    return jax.shard_map(
        functools.partial(shards, mesh.shape["frame"]),
        mesh=mesh,
        in_specs=(
            P("frame", "chan"),
            P("frame", "chan"),
            P("frame", "chan"),
            P(None, "chan", None),
            P("frame", "chan"),
        ),
        out_specs=P("frame", "chan"),
        check_vma=False,
    )
```

time: 155 us -> 73.4 us (0.47)
  the two profiles are of different devices: /device:TPU:16 before, /device:TPU:26 now
where the time goes in v1:
time: 73.4 us; the launch traced here: 73.2 us
  Pallas kernels  64.2 us (87%)
  local copies, waits for them, and re-layouts  9.02 us (12%)
    pallas_call x1, Pallas kernels, shards(): pl.pallas_call(functools.partial(kernel, frames), out_shape=jax.ShapeDtyp...  64.2 us
    unnamed x10, local copies, waits for them, and re-layouts  6.7 us
    pallas_call x1, local copies, waits for them, and re-layouts, shards(): pl.pallas_call(functools.partial(kernel, frames), out_shape=jax.ShapeDtyp...  2.32 us

profile of v1, /device:TPU:26, one launch (start us, length us, event | category | flops | bytes accessed | tf_op | source)
XLA Modules:
  0.0 73.2 jit_solution(9960902588001269703)
XLA Ops:
  0.0 0.0 copy-start
  0.0 2.4 %copy.6.q_ref = bf16[880,560]{1,0:T(8,128)(2,1)} copy(bf16[880,560]{0,1:T(8,128)(2,1)} %param.5) | data formatting | bytes 1971200 | tf_op args[0]
  2.4 0.0 copy-done
  2.4 0.0 copy-start.1
  2.4 1.4 %copy.7.k_ref = bf16[880,560]{1,0:T(8,128)(2,1)} copy(bf16[880,560]{0,1:T(8,128)(2,1)S(1)} %copy-done) | data formatting | bytes 1971200 | tf_op args[1]
  3.8 0.0 copy-done.1
  3.8 0.0 copy-start.2
  3.8 1.4 %copy.8.v_ref = bf16[880,560]{1,0:T(8,128)(2,1)} copy(bf16[880,560]{0,1:T(8,128)(2,1)S(1)} %copy-done.1) | data formatting | bytes 1971200 | tf_op args[2]
  5.3 0.0 copy-done.2
  5.3 1.4 %copy.9.g_hbm = bf16[880,560]{1,0:T(8,128)(2,1)} copy(bf16[880,560]{0,1:T(8,128)(2,1)S(1)} %copy-done.2) | data formatting | bytes 1971200 | tf_op args[4]
  6.7 64.2 %shard_map.55 = bf16[880,560]{1,0:T(8,128)(2,1)} custom-call(bf16[880,560]{1,0:T(8,128)(2,1)} %copy.6.q_ref, bf16[880,560]{1,0:T(8,128)(2,1)} %copy.7.k_ref, bf16[880,560]{1,0:T(8,128)(2,1)} %copy.8.v_ref, bf16[3,560,2240]{2,1,0:T(8,128)(2,1)} %w_hbm.1, bf16[880,560]{1,0:T(8,128)(2,1)} %copy.9.g_hbm), custom_call_target="tpu_custom_call" | custom-call | tf_op jit(solution)/shard_map/pallas_call | solution.py:315
  70.9 2.3 %copy.10 = bf16[880,560]{0,1:T(8,128)(2,1)} copy(bf16[880,560]{1,0:T(8,128)(2,1)} %shard_map.55) | data formatting | bytes 1971200 | tf_op jit(solution)/shard_map/pallas_call | solution.py:315
Async XLA Ops:
  0.0 2.4 %copy-start = (bf16[880,560]{0,1:T(8,128)(2,1)S(1)}, bf16[880,560]{0,1:T(8,128)(2,1)}, u32[]{:S(2)}) copy-start(bf16[880,560]{0,1:T(8,128)(2,1)} %param.6) | copy-start | bytes 2956804
  2.4 1.4 %copy-start.1 = (bf16[880,560]{0,1:T(8,128)(2,1)S(1)}, bf16[880,560]{0,1:T(8,128)(2,1)}, u32[]{:S(2)}) copy-start(bf16[880,560]{0,1:T(8,128)(2,1)} %param.7) | copy-start | bytes 2956804
  3.8 1.4 %copy-start.2 = (bf16[880,560]{0,1:T(8,128)(2,1)S(1)}, bf16[880,560]{0,1:T(8,128)(2,1)}, u32[]{:S(2)}) copy-start(bf16[880,560]{0,1:T(8,128)(2,1)} %param.9) | copy-start | bytes 2956804

commit v2 on v1

--- a/solution.py
+++ b/solution.py
@@ -9,7 +9,7 @@
 
 HD = 112
 TPF = 880
-PARTS = 2
+PARTS = 4
 F32 = jnp.float32
 BF16 = jnp.bfloat16
 MESH = pl.DeviceIdType.MESH
@@ -17,8 +17,8 @@
 
 def kernel(
     frames,
-    q_ref, k_ref, v_ref, w_hbm, g_hbm, out_ref,
-    w_all, wb, wsib, gate, own_state, pair_state, chain_in, chain_out, spread, qx,
+    q_hbm, k_hbm, v_hbm, w_hbm, g_hbm, out_ref,
+    turned, q_ref, w_all, wb, wsib, gate, own_state, pair_state, chain_in, chain_out, spread, qx,
     a_own, a_sib, cross, cross_in, kept, back, back_in,
     load_sem, w_send, w_recv, x_send, x_recv, c_send, c_recv, q_send, q_recv,
     s_send, s_recv, h_send, h_recv, f_send, f_recv, y_send, y_recv, b_send, b_recv,
@@ -46,12 +46,6 @@
             device_id=device, device_id_type=MESH,
         )
 
-    taps = w_hbm.shape[0]
-    loads = [pltpu.make_async_copy(w_hbm.at[t], w_all.at[t], load_sem.at[t]) for t in range(taps)]
-    loads.append(pltpu.make_async_copy(g_hbm, gate, load_sem.at[taps]))
-    for load in loads:
-        load.start()
-
     barrier = pltpu.get_barrier_semaphore()
     for device in (sib, far, mate):
         pl.semaphore_signal(barrier, inc=1, device_id=device, device_id_type=MESH)
@@ -64,20 +58,18 @@
     def _():
         pl.semaphore_signal(barrier, inc=1, device_id=down, device_id_type=MESH)
 
-    col_head = lax.broadcasted_iota(jnp.int32, (HD, width), 1) // HD
-    full = lax.dot_general(
-        jnp.maximum(k_ref[...], 0), v_ref[...], (((0,), (0,)), ((), ())),
-        preferred_element_type=F32,
-    )
-    state = jnp.zeros((HD, width), F32)
-    for h in range(heads):
-        state = jnp.where(col_head == h, full[h * HD:(h + 1) * HD, :], state)
-    own_state[...] = state.astype(BF16)
-
+    taps = w_hbm.shape[0]
+    moves = [
+        pltpu.make_async_copy(source, turned.at[i], load_sem.at[taps + i])
+        for i, source in enumerate((q_hbm, k_hbm, v_hbm, g_hbm))
+    ]
+    loads = [pltpu.make_async_copy(w_hbm.at[t], w_all.at[t], load_sem.at[t]) for t in range(taps)]
+    for load in moves + loads:
+        load.start()
+
+    moves[0].wait()
+    q_ref[...] = jnp.transpose(turned[0])
     pl.semaphore_wait(barrier, 3 + jnp.where(first, 0, 1) + jnp.where(last, 0, 1))
-
-    swap = remote(own_state, pair_state, x_send.at[0], x_recv.at[0], mate)
-    swap.start()
     mate_row = pl.multiple_of((1 - x) * shift, 16)
     q_moves = [
         remote(
@@ -86,7 +78,22 @@
         )
         for i in range(PARTS)
     ]
-    for move in q_moves:
+    q_moves[0].start()
+
+    col_head = lax.broadcasted_iota(jnp.int32, (HD, width), 1) // HD
+    moves[1].wait()
+    moves[2].wait()
+    full = lax.dot_general(
+        jnp.maximum(turned[1], 0), turned[2], (((1,), (1,)), ((), ())),
+        preferred_element_type=F32,
+    )
+    state = jnp.zeros((HD, width), F32)
+    for h in range(heads):
+        state = jnp.where(col_head == h, full[h * HD:(h + 1) * HD, :], state)
+    own_state[...] = state.astype(BF16)
+    swap = remote(own_state, pair_state, x_send.at[0], x_recv.at[0], mate)
+    swap.start()
+    for move in q_moves[1:]:
         move.start()
 
     for t in range(taps):
@@ -99,6 +106,9 @@
     ]
     for move in w_moves:
         move.start()
+
+    moves[3].wait()
+    gate[...] = jnp.transpose(turned[3])
 
     @pl.when(first)
     def _():
@@ -207,8 +217,12 @@
         u = gate[span, :].astype(F32)
         out_ref[span, :] = (total * (u / (1.0 + jnp.exp(-u)))).astype(BF16)
 
+    def place(s):
+        turn = s // PARTS
+        return x + (1 - turn) * (1 - 2 * x), lax.rem(s, PARTS)
+
     def finish(s):
-        j, i = s // PARTS, lax.rem(s, PARTS)
+        j, i = place(s)
         y_move(s).wait_recv()
         total = kept[s] + cross_in[s].astype(F32)
 
@@ -221,15 +235,14 @@
             back[i] = total.astype(BF16)
             b_move(i).start()
 
-    loads[taps].wait()
     w_moves[0].wait_recv()
     w_moves[1].wait_recv()
 
     def step(s, carry):
-        j, i = s // PARTS, lax.rem(s, PARTS)
+        j, i = place(s)
         span = pl.ds(pl.multiple_of(i * chunk, 16), chunk)
 
-        @pl.when(j == 0)
+        @pl.when(s < PARTS)
         def _():
             to_sib(1, i).wait_recv()
             to_sib(2, i).wait_recv()
@@ -315,9 +328,11 @@
     return pl.pallas_call(
         functools.partial(kernel, frames),
         out_shape=jax.ShapeDtypeStruct((rows, width), BF16),
-        in_specs=[vmem, vmem, vmem, hbm, hbm],
+        in_specs=[hbm] * 5,
         out_specs=vmem,
         scratch_shapes=[
+            pltpu.VMEM((4, width, rows), BF16),
+            pltpu.VMEM((rows, width), BF16),
             pltpu.VMEM((taps, width, outs), BF16),
             pltpu.VMEM((chans, taps, width, width), BF16),
             pltpu.VMEM((2, taps, width, width), BF16),
@@ -335,7 +350,7 @@
             pltpu.VMEM((2 * PARTS, chunk, width), F32),
             pltpu.VMEM((PARTS, chunk, width), BF16),
             pltpu.VMEM((PARTS, chunk, width), BF16),
-            dma((taps + 1,)),
+            dma((taps + 4,)),
             dma((2,)), dma((2,)),
             dma((1,)), dma((1,)),
             dma((2,)), dma((2,)),
@@ -349,7 +364,7 @@
         compiler_params=pltpu.CompilerParams(
             collective_id=0, has_side_effects=True, vmem_limit_bytes=56 * 1024 * 1024
         ),
-    )(query_act, key_act, value_act, conv_weight, gate_act)
+    )(query_act.T, key_act.T, value_act.T, conv_weight, gate_act.T)
 
 
 def solution(mesh):

time: 73.4 us -> 65.4 us (0.89)
  the two profiles are of different devices: /device:TPU:26 before, /device:TPU:16 now
where the time goes in v2:
time: 65.4 us; the launch traced here: 65.1 us
  Pallas kernels  62.8 us (96%)
  local copies, waits for them, and re-layouts  2.32 us (4%)
    pallas_call x1, Pallas kernels, shards(): pl.pallas_call(functools.partial(kernel, frames), out_shape=jax.ShapeDtyp...  62.8 us
    pallas_call x1, local copies, waits for them, and re-layouts, shards(): pl.pallas_call(functools.partial(kernel, frames), out_shape=jax.ShapeDtyp...  2.32 us

profile of v2, /device:TPU:16, one launch (start us, length us, event | category | flops | bytes accessed | tf_op | source)
XLA Modules:
  0.0 65.1 jit_solution(12483015642920540565)
XLA Ops:
  0.0 62.8 %shard_map.55 = bf16[880,560]{1,0:T(8,128)(2,1)} custom-call(bf16[560,880]{1,0:T(8,128)(2,1)} %bitcast.4, bf16[560,880]{1,0:T(8,128)(2,1)} %bitcast.5, bf16[560,880]{1,0:T(8,128)(2,1)} %bitcast.6, bf16[3,560,2240]{2,1,0:T(8,128)(2,1)} %w_hbm.1, bf16[560,880]{1,0:T(8,128)(2,1)} %bitcast.7), custom_call_target="tpu_custom_call" | custom-call | tf_op jit(solution)/shard_map/pallas_call | solution.py:328
  62.8 2.3 %copy.6 = bf16[880,560]{0,1:T(8,128)(2,1)} copy(bf16[880,560]{1,0:T(8,128)(2,1)} %shard_map.55) | data formatting | bytes 1971200 | tf_op jit(solution)/shard_map/pallas_call | solution.py:328

commit v3 on v2

--- a/solution.py
+++ b/solution.py
@@ -9,7 +9,8 @@
 
 HD = 112
 TPF = 880
-PARTS = 4
+PARTS = 2
+PIECES = 2
 F32 = jnp.float32
 BF16 = jnp.bfloat16
 MESH = pl.DeviceIdType.MESH
@@ -19,13 +20,14 @@
     frames,
     q_hbm, k_hbm, v_hbm, w_hbm, g_hbm, out_ref,
     turned, q_ref, w_all, wb, wsib, gate, own_state, pair_state, chain_in, chain_out, spread, qx,
-    a_own, a_sib, cross, cross_in, kept, back, back_in,
+    a_own, a_sib, cross, cross_in, kept, held, back, back_in,
     load_sem, w_send, w_recv, x_send, x_recv, c_send, c_recv, q_send, q_recv,
     s_send, s_recv, h_send, h_recv, f_send, f_recv, y_send, y_recv, b_send, b_recv,
 ):
     rows, width = q_ref.shape
     half = qx.shape[0]
     chunk = half // PARTS
+    piece = chunk // PIECES
     shift = rows - half
     heads = width // HD
     pairs = frames // 2
@@ -73,10 +75,10 @@
     mate_row = pl.multiple_of((1 - x) * shift, 16)
     q_moves = [
         remote(
-            q_ref.at[pl.ds(pl.multiple_of(mate_row + i * chunk, 16), chunk), :],
-            qx.at[pl.ds(i * chunk, chunk), :], q_send.at[i], q_recv.at[i], mate,
+            q_ref.at[pl.ds(pl.multiple_of(mate_row + i * piece, 16), piece), :],
+            qx.at[pl.ds(i * piece, piece), :], q_send.at[i], q_recv.at[i], mate,
         )
-        for i in range(PARTS)
+        for i in range(PARTS * PIECES)
     ]
     q_moves[0].start()
 
@@ -107,9 +109,6 @@
     for move in w_moves:
         move.start()
 
-    moves[3].wait()
-    gate[...] = jnp.transpose(turned[3])
-
     @pl.when(first)
     def _():
         a_own[0] = jnp.zeros((half, width), BF16)
@@ -189,22 +188,34 @@
 
     my_row = pl.multiple_of(x * shift, 16)
     for i in range(PARTS):
+        row = pl.multiple_of(my_row + i * chunk, 16)
+        a_own[1 + x, pl.ds(i * chunk, chunk), :] = attend(q_ref[pl.ds(row, chunk), :], spread[x])
+
+        @pl.when(jnp.logical_and(x == 0, jnp.logical_not(first)))
+        def _():
+            go_up(i).start()
+
+        @pl.when(jnp.logical_and(x == 1, jnp.logical_not(last)))
+        def _():
+            go_down(i).start()
+
+        to_sib(1 + x, i).start()
+
+    for i in range(PARTS):
         span = pl.ds(i * chunk, chunk)
-        mine = attend(q_ref[pl.ds(pl.multiple_of(my_row + i * chunk, 16), chunk), :], spread[x])
-        a_own[1 + x, span, :] = mine
-        q_moves[i].wait_recv()
+        for move in q_moves[i * PIECES:(i + 1) * PIECES]:
+            move.wait_recv()
         a_own[2 - x, span, :] = attend(qx[span, :], spread[1 - x])
 
-        @pl.when(jnp.logical_not(last))
+        @pl.when(jnp.logical_and(x == 1, jnp.logical_not(first)))
+        def _():
+            go_up(i).start()
+
+        @pl.when(jnp.logical_and(x == 0, jnp.logical_not(last)))
         def _():
             go_down(i).start()
 
-        @pl.when(jnp.logical_not(first))
-        def _():
-            go_up(i).start()
-
-        to_sib(1, i).start()
-        to_sib(2, i).start()
+        to_sib(2 - x, i).start()
 
     def y_move(s):
         return remote(cross.at[s], cross_in.at[s], y_send.at[s], y_recv.at[s], far)
@@ -259,20 +270,27 @@
 
         has = jnp.logical_and(p + j > 0, p + j < pairs)
 
+        held[...] = inner(wb.at[far_m], wsib.at[1])
+
         @pl.when(has)
         def _():
             remote(part(a_own, 2 - j, i), part(a_own, 3 * j, i), h_send.at[j, i], h_recv.at[j, i], sib).wait_recv()
             forward(j, i).start()
 
-        kept[s] = inner(wb.at[far_m], wsib.at[1])
+        kept[s] = inner(wb.at[m], wsib.at[0])
 
         @pl.when(has)
         def _():
             forward(j, i).wait_recv()
 
-        cross[s] = (kept[s] + outer(wb.at[far_m], wsib.at[1])).astype(BF16)
+        cross[s] = (held[...] + outer(wb.at[far_m], wsib.at[1])).astype(BF16)
         y_move(s).start()
-        kept[s] = inner(wb.at[m], wsib.at[0]) + outer(wb.at[m], wsib.at[0])
+        kept[s] += outer(wb.at[m], wsib.at[0])
+
+        @pl.when(s == 0)
+        def _():
+            moves[3].wait()
+            gate[...] = jnp.transpose(turned[3])
 
         @pl.when(s > 0)
         def _():
@@ -282,10 +300,10 @@
 
     steps = 2 * PARTS
     lax.fori_loop(0, steps, step, 0)
-    finish(steps - 1)
     for i in range(PARTS):
         b_move(i).wait_recv()
         gated(back_in[i].astype(F32), mate_row + i * chunk)
+    finish(steps - 1)
 
     for move in q_moves:
         move.wait_send()
@@ -320,7 +338,7 @@
     taps, _, outs = conv_weight.shape
     chans = outs // width
     assert rows == TPF and frames % 2 == 0 and chans == 4
-    half = -(-rows // (32 * PARTS)) * 16 * PARTS
+    half = -(-rows // (32 * PARTS * PIECES)) * 16 * PARTS * PIECES
     chunk = half // PARTS
     dma = pltpu.SemaphoreType.DMA
     vmem = pl.BlockSpec(memory_space=pltpu.VMEM)
@@ -348,13 +366,14 @@
             pltpu.VMEM((2 * PARTS, chunk, width), BF16),
             pltpu.VMEM((2 * PARTS, chunk, width), BF16),
             pltpu.VMEM((2 * PARTS, chunk, width), F32),
+            pltpu.VMEM((chunk, width), F32),
             pltpu.VMEM((PARTS, chunk, width), BF16),
             pltpu.VMEM((PARTS, chunk, width), BF16),
             dma((taps + 4,)),
             dma((2,)), dma((2,)),
             dma((1,)), dma((1,)),
             dma((2,)), dma((2,)),
-            dma((PARTS,)), dma((PARTS,)),
+            dma((PARTS * PIECES,)), dma((PARTS * PIECES,)),
             dma((2, PARTS)), dma((2, PARTS)),
             dma((2, PARTS)), dma((2, PARTS)),
             dma((2, PARTS)), dma((2, PARTS)),

time: 65.4 us -> 63.1 us (0.965)
  Pallas kernels: 62.8 us -> 60.6 us
    pallas_call x1, Pallas kernels: 62.8 us -> 60.6 us  [shards(): pl.pallas_call(functools.partial(kernel, frames), out_shape=jax.ShapeDtyp...]
where the time goes in v3:
time: 63.1 us; the launch traced here: 63 us
  Pallas kernels  60.6 us (96%)
  local copies, waits for them, and re-layouts  2.32 us (4%)
    pallas_call x1, Pallas kernels, shards(): pl.pallas_call(functools.partial(kernel, frames), out_shape=jax.ShapeDtyp...  60.6 us
    pallas_call x1, local copies, waits for them, and re-layouts, shards(): pl.pallas_call(functools.partial(kernel, frames), out_shape=jax.ShapeDtyp...  2.32 us

profile of v3, /device:TPU:16, one launch (start us, length us, event | category | flops | bytes accessed | tf_op | source)
XLA Modules:
  0.0 63.0 jit_solution(10690986452317384846)
XLA Ops:
  0.0 60.6 %shard_map.55 = bf16[880,560]{1,0:T(8,128)(2,1)} custom-call(bf16[560,880]{1,0:T(8,128)(2,1)} %bitcast.4, bf16[560,880]{1,0:T(8,128)(2,1)} %bitcast.5, bf16[560,880]{1,0:T(8,128)(2,1)} %bitcast.6, bf16[3,560,2240]{2,1,0:T(8,128)(2,1)} %w_hbm.1, bf16[560,880]{1,0:T(8,128)(2,1)} %bitcast.7), custom_call_target="tpu_custom_call" | custom-call | tf_op jit(solution)/shard_map/pallas_call | solution.py:346
  60.7 2.3 %copy.6 = bf16[880,560]{0,1:T(8,128)(2,1)} copy(bf16[880,560]{1,0:T(8,128)(2,1)} %shard_map.55) | data formatting | bytes 1971200 | tf_op jit(solution)/shard_map/pallas_call | solution.py:346

commit v4 on v3

--- a/solution.py
+++ b/solution.py
@@ -186,19 +186,22 @@
     def forward(j, i):
         return remote(part(a_own, 3 * j, i), part(a_sib, 3 * j, i), f_send.at[j, i], f_recv.at[j, i], sib)
 
+    def halo_out(i):
+        @pl.when(jnp.logical_and(x == 0, jnp.logical_not(first)))
+        def _():
+            go_up(i).start()
+
+        @pl.when(jnp.logical_and(x == 1, jnp.logical_not(last)))
+        def _():
+            go_down(i).start()
+
     my_row = pl.multiple_of(x * shift, 16)
     for i in range(PARTS):
         row = pl.multiple_of(my_row + i * chunk, 16)
         a_own[1 + x, pl.ds(i * chunk, chunk), :] = attend(q_ref[pl.ds(row, chunk), :], spread[x])
 
-        @pl.when(jnp.logical_and(x == 0, jnp.logical_not(first)))
-        def _():
-            go_up(i).start()
-
-        @pl.when(jnp.logical_and(x == 1, jnp.logical_not(last)))
-        def _():
-            go_down(i).start()
-
+        if i == 0:
+            halo_out(0)
         to_sib(1 + x, i).start()
 
     for i in range(PARTS):
@@ -276,6 +279,11 @@
         def _():
             remote(part(a_own, 2 - j, i), part(a_own, 3 * j, i), h_send.at[j, i], h_recv.at[j, i], sib).wait_recv()
             forward(j, i).start()
+
+        @pl.when(s == 0)
+        def _():
+            for later in range(1, PARTS):
+                halo_out(later)
 
         kept[s] = inner(wb.at[m], wsib.at[0])
 

time: 63.1 us -> 63.5 us (level)
  no operation moved by 1% of the time
where the time goes in v4:
time: 63.5 us; the launch traced here: 63.3 us
  Pallas kernels  61 us (96%)
  local copies, waits for them, and re-layouts  2.32 us (4%)
    pallas_call x1, Pallas kernels, shards(): pl.pallas_call(functools.partial(kernel, frames), out_shape=jax.ShapeDtyp...  61 us
    pallas_call x1, local copies, waits for them, and re-layouts, shards(): pl.pallas_call(functools.partial(kernel, frames), out_shape=jax.ShapeDtyp...  2.32 us

profile of v4, /device:TPU:16, one launch (start us, length us, event | category | flops | bytes accessed | tf_op | source)
XLA Modules:
  0.0 63.3 jit_solution(12873153991862924382)
XLA Ops:
  0.0 61.0 %shard_map.55 = bf16[880,560]{1,0:T(8,128)(2,1)} custom-call(bf16[560,880]{1,0:T(8,128)(2,1)} %bitcast.4, bf16[560,880]{1,0:T(8,128)(2,1)} %bitcast.5, bf16[560,880]{1,0:T(8,128)(2,1)} %bitcast.6, bf16[3,560,2240]{2,1,0:T(8,128)(2,1)} %w_hbm.1, bf16[560,880]{1,0:T(8,128)(2,1)} %bitcast.7), custom_call_target="tpu_custom_call" | custom-call | tf_op jit(solution)/shard_map/pallas_call | solution.py:354
  61.0 2.3 %copy.6 = bf16[880,560]{0,1:T(8,128)(2,1)} copy(bf16[880,560]{1,0:T(8,128)(2,1)} %shard_map.55) | data formatting | bytes 1971200 | tf_op jit(solution)/shard_map/pallas_call | solution.py:354
